TPU v7x, 32 devices: a whole 2x2x4 slice. The times are simulated.
32 devices in a mesh: rg: 4 (over y, core), az: 8 (over z, x).
Axes of the slice: x: 2, y: 2, z: 4, core: 2. Of those that a mesh axis runs over, the one named last changes fastest.
Arguments:
- raw_pulses: bfloat16 [2, 2048, 65536], P(None, ('rg', 'az')), may hold values from -6 to 6
- range_phase: float32 [65536], replicated, may hold values from -3.140625 to 3.140625
- azimuth_rate: float32 [65536], P(('rg', 'az')), may hold values from 40 to 400
- conc_azimuth: float32 [2048], replicated, may hold values from 0.2 to 1
- conc_range: float32 [65536], replicated, may hold values from 0.2 to 1
Outputs:
- edge_azimuth: float32 [2048, 65536], P(None, ('rg', 'az'))
- edge_range: float32 [2048, 65536], P(('rg', 'az'))
All inputs are finite; a program needn't handle non-finite values.
Results may differ from a plain program's by a relative error of at most 0.028.
Values may be sent and summed in bfloat16 or wider, within the bound.
A program may use at most 192 MiB of HBM per device.

v0:
```python
import math

import jax
import jax.numpy as jnp
from jax import lax
from jax.sharding import PartitionSpec as P

RA = 256
RB = 256
QA = 32
QB = 64


def dft_table(length, sign):
    indices = jnp.arange(length, dtype=jnp.int32)
    product = indices[:, None] * indices[None, :] % length
    angles = sign * 2.0 * math.pi / length * product.astype(jnp.float32)
    factor = 1.0 / math.sqrt(length)
    return (
        (jnp.cos(angles) * factor).astype(jnp.bfloat16),
        (jnp.sin(angles) * factor).astype(jnp.bfloat16),
    )


def twiddle(first_len, second, sign):
    length_all = first_len * second
    product = (
        jnp.arange(first_len, dtype=jnp.int32)[:, None]
        * jnp.arange(second, dtype=jnp.int32)[None, :]
        % length_all
    )
    angles = sign * 2.0 * math.pi / length_all * product.astype(jnp.float32)
    return (jnp.cos(angles), jnp.sin(angles))


def signed_freq(first_len, second):
    length_all = first_len * second
    freqs = (
        jnp.arange(first_len, dtype=jnp.int32)[:, None]
        + first_len * jnp.arange(second, dtype=jnp.int32)[None, :]
    )
    return jnp.where(freqs < length_all // 2, freqs, freqs - length_all)


def product_of(form, matrix, values):
    return jnp.einsum(form, matrix, values, preferred_element_type=jnp.float32)


def contract(form, matrix, pieces):
    if len(pieces) == 1:
        return (product_of(form, matrix[0], pieces[0]), product_of(form, matrix[1], pieces[0]))
    return (
        product_of(form, matrix[0], pieces[0]) - product_of(form, matrix[1], pieces[1]),
        product_of(form, matrix[0], pieces[1]) + product_of(form, matrix[1], pieces[0]),
    )


def rotate(pieces, cosine, sine_part):
    return (pieces[0] * cosine - pieces[1] * sine_part, pieces[0] * sine_part + pieces[1] * cosine)


def to_half(pieces):
    return tuple((piece.astype(jnp.bfloat16) for piece in pieces))


def forward(pieces, first_len, second, forms, expand):
    sectioned = contract(forms[0], dft_table(first_len, -1.0), pieces)
    cosine, sine_part = twiddle(first_len, second, -1.0)
    sectioned = to_half(rotate(sectioned, expand(cosine), expand(sine_part)))
    return contract(forms[1], dft_table(second, -1.0), sectioned)


def inverse(pieces, first_len, second, forms, expand, real_only):
    sectioned = contract(forms[2], dft_table(second, 1.0), pieces)
    cosine, sine_part = twiddle(first_len, second, 1.0)
    sectioned = to_half(rotate(sectioned, expand(cosine), expand(sine_part)))
    if real_only:
        mat_real, mat_imag = dft_table(first_len, 1.0)
        return product_of(forms[3], mat_real, sectioned[0]) - product_of(
            forms[3], mat_imag, sectioned[1]
        )
    return contract(forms[3], dft_table(first_len, 1.0), sectioned)


def range_forms():
    return ("kn,pnb->pkb", "bm,pkb->pkm", "mb,pkm->pkb", "nk,pkb->pnb")


def azimuth_forms():
    return ("ka,abr->kbr", "bm,kbr->kmr", "mb,kmr->kbr", "nk,kbr->nbr")


def range_expand(table):
    return table[None]


def azimuth_expand(table):
    return table[:, :, None]


def concentrate(values, first_len, second, factors, forms, expand):
    spectrum = forward((values,), first_len, second, forms, expand)
    signs = jnp.sign(signed_freq(first_len, second)).astype(jnp.float32)
    weights = expand(signs * factors.reshape(second, first_len).T)
    jumped = to_half((-weights * spectrum[1], weights * spectrum[0]))
    return inverse(jumped, first_len, second, forms, expand, True)


def range_compress(pieces, range_phase):
    count = pieces[0].shape[0]
    shaped = tuple((piece.reshape(count, RA, RB) for piece in pieces))
    spectrum = forward(shaped, RA, RB, range_forms(), range_expand)
    grid = range_phase.reshape(RB, RA).T
    spectrum = to_half(rotate(spectrum, jnp.cos(grid)[None], jnp.sin(grid)[None]))
    result = inverse(spectrum, RA, RB, range_forms(), range_expand, False)
    return tuple((piece.astype(jnp.bfloat16).reshape(count, RA * RB) for piece in result))


def azimuth_part(pieces, rates, conc_azimuth):
    width = pieces[0].shape[1]
    shaped = tuple((piece.reshape(QA, QB, width) for piece in pieces))
    spectrum = forward(shaped, QA, QB, azimuth_forms(), azimuth_expand)
    signed = signed_freq(QA, QB).astype(jnp.float32) / (QA * QB)
    phases = rates[None, None, :] * (signed * signed)[:, :, None]
    spectrum = to_half(rotate(spectrum, jnp.cos(phases), jnp.sin(phases)))
    picture = inverse(spectrum, QA, QB, azimuth_forms(), azimuth_expand, False)
    magnitude = jnp.sqrt(picture[0] * picture[0] + picture[1] * picture[1]).astype(jnp.bfloat16)
    edges = concentrate(magnitude, QA, QB, conc_azimuth, azimuth_forms(), azimuth_expand)
    return (edges.reshape(QA * QB, width), magnitude.reshape(QA * QB, width))


def on_device(raw_pulses, range_phase, azimuth_rate, conc_azimuth, conc_range):
    local_pulses = raw_pulses.shape[1]
    compressed = jnp.stack(range_compress((raw_pulses[0], raw_pulses[1]), range_phase))
    turned = lax.all_to_all(compressed, ("rg", "az"), split_axis=2, concat_axis=1, tiled=True)
    edge_azimuth, magnitude = azimuth_part((turned[0], turned[1]), azimuth_rate, conc_azimuth)
    rows = lax.all_to_all(magnitude, ("rg", "az"), split_axis=0, concat_axis=1, tiled=True)
    edges = concentrate(
        rows.reshape(local_pulses, RA, RB), RA, RB, conc_range, range_forms(), range_expand
    )
    edge_range = edges.reshape(local_pulses, RA * RB)
    return (edge_azimuth, edge_range)


def solution(mesh):
    in_specs = (P(None, ("rg", "az"), None), P(), P(("rg", "az")), P(), P())
    out_specs = (P(None, ("rg", "az")), P(("rg", "az"), None))
    return jax.shard_map(
        on_device, mesh=mesh, in_specs=in_specs, out_specs=out_specs, check_vma=False
    )
```

profile of v0, /device:TPU:0, one launch (start us, length us, event | category | flops | bytes accessed | tf_op | source)
XLA Modules:
  0.0 1731.9 jit_solution(16001821360271386088)
XLA Ops:
  70.1 18.5 %fusion.12 = (bf16[64,256,256]{2,1,0:T(8,128)(2,1)S(1)}, bf16[64,256,256]{2,1,0:T(8,128)(2,1)}) fusion(f32[256,64,256]{2,0,1:T(8,128)} %convolution_add_fusion.3, f32[256,256]{1,0:T(8,128)S(1)} %get-tuple-element.29, f32[256,256]{1,0:T(8,128)S(1)} %get-tuple-element.30, f32[256,64,256]{2,0,1:T(8,128)} %fusion.124, bf16[64,256,256]{2,1,0:T(8,128)(2,1)} %bitcast.226), kind=kOutput, calls=%fused_computation.51 | convolution fusion | flops 2186280960 | bytes 59244544 | tf_op jit(solution)/shard_map/kn,pnb->pkb/dot_general | solution.py:46
  125.4 30.6 %subtract_convert_fusion.7 = (bf16[64,256,256]{2,1,0:T(8,128)(2,1)S(1)}, bf16[64,256,256]{2,1,0:T(8,128)(2,1)}) fusion(f32[64,256,256]{2,1,0:T(8,128)} %convolution_subtract_fusion.2, f32[256,256]{1,0:T(8,128)S(1)} %copy.167, f32[256,256]{1,0:T(8,128)S(1)} %copy.166, f32[64,256,256]{2,1,0:T(8,128)} %fusion.118, bf16[64,256,256]{2,1,0:T(8,128)(2,1)} %copy-done.1), kind=kOutput, calls=%fused_computation.40 | convolution fusion | flops 2186280960 | bytes 59244544 | tf_op jit(solution)/shard_map/bm,pkb->pkm/dot_general | solution.py:46
  192.7 19.0 %subtract_convert_fusion.6 = (bf16[64,256,256]{2,1,0:T(8,128)(2,1)}, bf16[64,256,256]{2,1,0:T(8,128)(2,1)}) fusion(f32[64,256,256]{2,1,0:T(8,128)} %convolution_subtract_fusion.1, f32[256,256]{1,0:T(8,128)S(1)} %copy-done.10, f32[256,256]{1,0:T(8,128)S(1)} %copy-done.12, f32[64,256,256]{2,1,0:T(8,128)} %fusion.100, ...), kind=kOutput, calls=%fused_computation.38 | convolution fusion | flops 2186280960 | bytes 59244544 | tf_op jit(solution)/shard_map/mb,pkm->pkb/dot_general | solution.py:46
  319.0 66.6 %copy.174 = bf16[2,64,65536]{1,0,2:T(2,128)(2,1)} copy(bf16[2,64,65536]{2,1,0:T(8,128)(2,1)} %pad_maximum_fusion) | data formatting | bytes 33554432 | tf_op jit(solution)/shard_map/stack | solution.py:134
  385.7 37.9 %reshape.207 = bf16[32,2,131072]{2,1,0:T(2,128)(2,1)} reshape(bf16[65536,2,64]{2,1,0:T(2,128)(2,1)} %bitcast.223) | data formatting | bytes 33554432
  432.4 368.0 %all-to-all-done = bf16[32,2,131072]{2,1,0:T(2,128)(2,1)} async-done(((bf16[32,2,131072]{2,1,0:T(2,128)(2,1)}), bf16[32,2,131072]{2,1,0:T(2,128)(2,1)}, u32[]{:S(2)}, u32[]{:S(2)}) %all-to-all-start) | async-done | bytes 16777248 | tf_op jit(solution)/shard_map/all_to_all | solution.py:135
  800.4 36.9 %reshape.208 = bf16[65536,2,64]{2,1,0:T(2,128)(2,1)} reshape(bf16[32,2,131072]{2,1,0:T(2,128)(2,1)} %all-to-all-done) | data formatting | bytes 33554432
  837.4 50.6 %copy.220 = bf16[2,64,32,2048]{3,2,1,0:T(8,128)(2,1)} copy(bf16[2,64,32,2048]{1,0,3,2:T(2,128)(2,1)} %bitcast.224) | data formatting | bytes 33554432 | tf_op jit(solution)/shard_map/all_to_all | solution.py:135
  917.3 26.9 %subtract_convert_fusion.4 = (bf16[32,64,2048]{2,0,1:T(8,128)(2,1)}, bf16[32,64,2048]{2,0,1:T(8,128)(2,1)}) fusion(f32[32,64]{0,1:T(8,128)S(1)} %copy.177, f32[32,64]{0,1:T(8,128)S(1)} %copy.176, f32[32,64,2048]{2,0,1:T(8,128)} %fusion.29, f32[32,64,2048]{2,0,1:T(8,128)} %fusion.30, f32[32,64,2048]{2,0,1:T(8,128)} %fusion.32, ...), kind=kOutput, calls=%fused_computation.34 | convolution fusion | flops 310394880 | bytes 75513856 | tf_op jit(solution)/shard_map/ka,abr->kbr/dot_general | solution.py:46
  944.2 20.6 %fusion.55 = f32[32,2048,64]{1,2,0:T(8,128)} fusion(bf16[32,64,2048]{2,0,1:T(8,128)(2,1)} %get-tuple-element.6), kind=kOutput, calls=%fused_computation.96 | convolution fusion | flops 536936448 | bytes 25165824 | tf_op jit(solution)/shard_map/bm,kbr->kmr/dot_general | solution.py:46
  999.2 77.8 %fusion.5 = (bf16[32,64,2048]{2,1,0:T(8,128)(2,1)S(1)}, bf16[32,64,2048]{2,1,0:T(8,128)(2,1)S(1)}) fusion(f32[32,64]{1,0:T(8,128)S(1)} %get-tuple-element.28, f32[2048]{0:T(1024)S(1)} %copy-done.22, f32[32,2048,64]{1,2,0:T(8,128)} %fusion.55, f32[32,2048,64]{1,2,0:T(8,128)} %fusion.53, f32[32,2048,64]{1,2,0:T(8,128)} %fusion.49, ...), kind=kOutput, calls=%fused_computation.7 | convolution fusion | flops 583008256 | bytes 75522048 | tf_op jit(solution)/shard_map/bm,kbr->kmr/dot_general | solution.py:46
  1102.8 26.4 %fusion.14 = (bf16[32,64,2048]{2,1,0:T(8,128)(2,1)}, bf16[32,64,2048]{2,1,0:T(8,128)(2,1)}) fusion(f32[32,64]{1,0:T(8,128)S(1)} %get-tuple-element.33, f32[32,64]{1,0:T(8,128)S(1)} %get-tuple-element.34, f32[32,2048,64]{1,2,0:T(8,128)} %fusion.141, f32[32,2048,64]{1,2,0:T(8,128)} %fusion.147, f32[32,2048,64]{1,2,0:T(8,128)} %fusion.139, ...), kind=kOutput, calls=%fused_computation.53 | convolution fusion | flops 578879488 | bytes 75513856 | tf_op jit(solution)/shard_map/mb,kmr->kbr/dot_general | solution.py:46
  1129.2 21.5 %fusion.41 = f32[32,64,2048]{2,0,1:T(8,128)} fusion(bf16[32,64,2048]{2,1,0:T(8,128)(2,1)} %get-tuple-element.11), kind=kOutput, calls=%fused_computation.82 | convolution fusion | flops 268451840 | bytes 25165824 | tf_op jit(solution)/shard_map/nk,kbr->nbr/dot_general | solution.py:46
  1168.7 18.1 %fusion.45 = f32[32,64,2048]{2,0,1:T(8,128)} fusion(bf16[32,64,2048]{2,1,0:T(8,128)(2,1)S(1)} %bitcast.236), kind=kOutput, calls=%fused_computation.86 | convolution fusion | flops 268451840 | bytes 25165824 | tf_op jit(solution)/shard_map/nk,kbr->nbr/dot_general | solution.py:46
  1186.9 48.9 %sqrt_convert_fusion = bf16[32,64,2048]{2,0,1:T(8,128)(2,1)} fusion(f32[32,64,2048]{2,0,1:T(8,128)} %fusion.41, f32[32,64,2048]{2,0,1:T(8,128)} %fusion.45, f32[32,64,2048]{2,0,1:T(8,128)} %fusion.43, bf16[32,64,2048]{2,1,0:T(8,128)(2,1)} %get-tuple-element.10), kind=kOutput, calls=%fused_computation.30 | convolution fusion | flops 293617664 | bytes 67108864 | tf_op jit(solution)/shard_map/nk,kbr->nbr/dot_general | solution.py:46
  1291.5 20.5 %fusion.33 = f32[32,2048,64]{1,2,0:T(8,128)} fusion(bf16[32,64,2048]{2,0,1:T(8,128)(2,1)} %get-tuple-element.23), kind=kOutput, calls=%fused_computation.74 | convolution fusion | flops 536936448 | bytes 25165824 | tf_op jit(solution)/shard_map/bm,kbr->kmr/dot_general | solution.py:46
  1312.0 28.8 %fusion.16 = bf16[32,64,2048]{2,1,0:T(8,128)(2,1)} fusion(f32[32,2048,64]{1,2,0:T(8,128)} %fusion.33, f32[32,64]{1,0:T(8,128)S(1)} %copy-done.24, bf16[32,64,2048]{2,0,1:T(8,128)(2,1)} %get-tuple-element.22), kind=kOutput, calls=%fused_computation.55 | convolution fusion | flops 549519360 | bytes 33562624 | tf_op jit(solution)/shard_map/bm,kbr->kmr/dot_general | solution.py:46
  1378.6 28.6 %fusion.17 = bf16[32,64,2048]{2,1,0:T(8,128)(2,1)} fusion(f32[32,2048,64]{1,2,0:T(8,128)} %fusion.35, f32[32,64]{1,0:T(8,128)S(1)} %copy-done.23, bf16[32,64,2048]{2,0,1:T(8,128)(2,1)} %get-tuple-element.22), kind=kOutput, calls=%fused_computation.56 | convolution fusion | flops 549519360 | bytes 33562624 | tf_op jit(solution)/shard_map/bm,kbr->kmr/dot_general | solution.py:46
  1418.8 26.2 %fusion.18 = (bf16[32,64,2048]{2,1,0:T(8,128)(2,1)}, bf16[32,64,2048]{2,1,0:T(8,128)(2,1)}) fusion(f32[32,64]{1,0:T(8,128)S(1)} %get-tuple-element.33, f32[32,64]{1,0:T(8,128)S(1)} %get-tuple-element.34, f32[32,2048,64]{1,2,0:T(8,128)} %fusion.145, f32[32,2048,64]{1,2,0:T(8,128)} %fusion.151, f32[32,2048,64]{1,2,0:T(8,128)} %fusion.143, ...), kind=kOutput, calls=%fused_computation.57 | convolution fusion | flops 578879488 | bytes 75513856 | tf_op jit(solution)/shard_map/mb,kmr->kbr/dot_general | solution.py:46
  1445.0 21.2 %fusion.21 = f32[32,64,2048]{2,0,1:T(8,128)} fusion(bf16[32,64,2048]{2,1,0:T(8,128)(2,1)} %get-tuple-element.9), kind=kOutput, calls=%fused_computation.62 | convolution fusion | flops 268451840 | bytes 25165824 | tf_op jit(solution)/shard_map/nk,kbr->nbr/dot_general | solution.py:46
  1466.2 26.5 %fusion.57 = f32[32,64,2048]{2,0,1:T(8,128)} fusion(f32[32,64,2048]{2,0,1:T(8,128)} %fusion.21, bf16[32,64,2048]{2,1,0:T(8,128)(2,1)} %get-tuple-element.8), kind=kOutput, calls=%fused_computation.98 | convolution fusion | flops 272646144 | bytes 41943040 | tf_op jit(solution)/shard_map/nk,kbr->nbr/dot_general | solution.py:46
  1492.8 18.1 %copy.192 = f32[32,64,2048]{2,1,0:T(8,128)} copy(f32[32,64,2048]{2,0,1:T(8,128)} %fusion.57) | data formatting | bytes 33554432 | tf_op jit(solution)/shard_map/sub | solution.py:79
  1667.4 21.9 %fusion.20 = f32[64,256,256]{2,1,0:T(8,128)} fusion(f32[64,256,256]{2,1,0:T(8,128)} %convolution_add_fusion, f32[64,256,256]{2,1,0:T(8,128)} %convolution_subtract_fusion, f32[256,256]{1,0:T(8,128)S(1)} %copy-done.11, f32[256,256]{1,0:T(8,128)S(1)} %copy-done.13), kind=kOutput, calls=%fused_computation.59 | convolution fusion | flops 2165309440 | bytes 50855936 | tf_op jit(solution)/shard_map/nk,pkb->pnb/dot_general | solution.py:46
  1689.3 24.6 %subtract_bitcast_fusion = f32[64,256,256]{1,2,0:T(8,128)} fusion(f32[64,256,256]{2,1,0:T(8,128)} %fusion.20, f32[64,256,256]{2,1,0:T(8,128)} %convolution_add_fusion, f32[64,256,256]{2,1,0:T(8,128)} %convolution_subtract_fusion, f32[256,256]{1,0:T(8,128)S(1)} %copy-done.11, f32[256,256]{1,0:T(8,128)S(1)} %copy-done.13), kind=kOutput, calls=%fused_computation.19 | convolution fusion | flops 2169503744 | bytes 67633152 | tf_op jit(solution)/shard_map/nk,pkb->pnb/dot_general | solution.py:46
  (154 shorter events, 645.3 us)
Async XLA Ops:
  1.7 68.4 %copy-start.14 = (f32[256,256]{1,0:T(8,128)}, f32[256,256]{1,0:T(8,128)S(1)}, u32[]{:S(2)}) copy-start(f32[256,256]{1,0:T(8,128)S(1)} %get-tuple-element.29) | copy-start | bytes 786436
  1.7 68.4 %copy-start.16 = (f32[256,256]{1,0:T(8,128)}, f32[256,256]{1,0:T(8,128)S(1)}, u32[]{:S(2)}) copy-start(f32[256,256]{1,0:T(8,128)S(1)} %get-tuple-element.30) | copy-start | bytes 786436
  108.8 15.3 copy-start.20
  175.0 17.7 %copy-start.10 = (f32[256,256]{1,0:T(8,128)S(1)}, f32[256,256]{1,0:T(8,128)}, u32[]{:S(2)}) copy-start(f32[256,256]{1,0:T(8,128)} %get-tuple-element.31) | copy-start | bytes 786436
  175.0 17.7 %copy-start.12 = (f32[256,256]{1,0:T(8,128)S(1)}, f32[256,256]{1,0:T(8,128)}, u32[]{:S(2)}) copy-start(f32[256,256]{1,0:T(8,128)} %get-tuple-element.32) | copy-start | bytes 786436
  423.6 376.8 %all-to-all-start = ((bf16[32,2,131072]{2,1,0:T(2,128)(2,1)}), bf16[32,2,131072]{2,1,0:T(2,128)(2,1)}, u32[]{:S(2)}, u32[]{:S(2)}) async-start(bf16[32,2,131072]{2,1,0:T(2,128)(2,1)} %reshape.207), calls=%async_computation | async-start | bytes 33554432 | tf_op jit(solution)/shard_map/all_to_all | solution.py:135
  944.2 20.7 %slice-start.8 = ((s8[8388608]{0:T(1024)(128)(4,1)}), s8[4194304]{0:T(1024)(128)(4,1)S(1)}, s32[]{:S(2)}) async-start(s8[8388608]{0:T(1024)(128)(4,1)} %bitcast.237), calls=%async_computation.10 | async-start | bytes 8388608
  944.2 20.7 %slice-start.9 = ((s8[8388608]{0:T(1024)(128)(4,1)}), s8[4194304]{0:T(1024)(128)(4,1)S(1)}, s32[]{:S(2)}) async-start(s8[8388608]{0:T(1024)(128)(4,1)} %bitcast.237), calls=%async_computation.11 | async-start | bytes 8388608
  944.2 38.0 %slice-start = ((s8[8388608]{0:T(1024)(128)(4,1)}), s8[4194304]{0:T(1024)(128)(4,1)S(1)}, s32[]{:S(2)}) async-start(s8[8388608]{0:T(1024)(128)(4,1)} %bitcast.229), calls=%async_computation.2 | async-start | bytes 8388608
  964.9 17.3 slice-start.1
  982.2 17.0 copy-start.22
  1077.0 17.5 %copy-start.8 = (bf16[32,64,2048]{2,1,0:T(8,128)(2,1)}, bf16[32,64,2048]{2,1,0:T(8,128)(2,1)S(1)}, u32[]{:S(2)}) copy-start(bf16[32,64,2048]{2,1,0:T(8,128)(2,1)S(1)} %get-tuple-element.13) | copy-start | bytes 25165828
  1129.2 21.5 %slice-start.4 = ((s8[8388608]{0:T(1024)(128)(4,1)}), s8[4194304]{0:T(1024)(128)(4,1)S(1)}, s32[]{:S(2)}) async-start(s8[8388608]{0:T(1024)(128)(4,1)} %bitcast.233), calls=%async_computation.6 | async-start | bytes 8388608
  1129.2 21.5 %slice-start.5 = ((s8[8388608]{0:T(1024)(128)(4,1)}), s8[4194304]{0:T(1024)(128)(4,1)S(1)}, s32[]{:S(2)}) async-start(s8[8388608]{0:T(1024)(128)(4,1)} %bitcast.233), calls=%async_computation.7 | async-start | bytes 8388608
  1129.2 39.5 %slice-start.6 = ((s8[8388608]{0:T(1024)(128)(4,1)}), s8[4194304]{0:T(1024)(128)(4,1)S(1)}, s32[]{:S(2)}) async-start(s8[8388608]{0:T(1024)(128)(4,1)} %bitcast.235), calls=%async_computation.8 | async-start | bytes 8388608
  1150.7 18.0 %slice-start.7 = ((s8[8388608]{0:T(1024)(128)(4,1)}), s8[4194304]{0:T(1024)(128)(4,1)S(1)}, s32[]{:S(2)}) async-start(s8[8388608]{0:T(1024)(128)(4,1)} %bitcast.235), calls=%async_computation.9 | async-start | bytes 8388608
  1235.8 27.0 %copy-start.17 = (f32[256,256]{1,0:T(8,128)S(1)}, f32[256,256]{1,0:T(8,128)}, u32[]{:S(2)}) copy-start(f32[256,256]{1,0:T(8,128)} %copy-done.16) | copy-start | bytes 786436
  1235.8 27.1 %copy-start.15 = (f32[256,256]{1,0:T(8,128)S(1)}, f32[256,256]{1,0:T(8,128)}, u32[]{:S(2)}) copy-start(f32[256,256]{1,0:T(8,128)} %copy-done.14) | copy-start | bytes 786436
  1235.8 27.2 %copy-start.21 = (f32[65536]{0:T(1024)S(1)}, f32[65536]{0:T(1024)}, u32[]{:S(2)}) copy-start(f32[65536]{0:T(1024)} %param.9) | copy-start | bytes 786436
  1247.2 263.8 %all-to-all-start.1 = ((bf16[32,64,2048]{2,1,0:T(8,128)(2,1)}), bf16[32,64,2048]{2,1,0:T(8,128)(2,1)}, u32[]{:S(2)}, u32[]{:S(2)}) async-start(bf16[32,64,2048]{2,1,0:T(8,128)(2,1)} %copy.194), calls=%async_computation.1 | async-start | bytes 16777216 | tf_op jit(solution)/shard_map/all_to_all | solution.py:137
  1291.4 20.5 %copy-start.24 = (f32[32,64]{1,0:T(8,128)S(1)}, f32[32,64]{1,0:T(8,128)}, u32[]{:S(2)}) copy-start(f32[32,64]{1,0:T(8,128)} %get-tuple-element.4) | copy-start | bytes 24580
  1340.8 20.8 %slice-start.2 = ((s8[8388608]{0:T(1024)(128)(4,1)}), s8[4194304]{0:T(1024)(128)(4,1)S(1)}, s32[]{:S(2)}) async-start(s8[8388608]{0:T(1024)(128)(4,1)} %bitcast.231), calls=%async_computation.4 | async-start | bytes 8388608
  1361.6 16.9 copy-start.23
  1652.2 15.2 copy-start.13
  (14 other events, 154.3 us)
where the time goes:
time: 1750 us; the launch traced here: 1730 us
  matrix products  979 us (56%)
  waiting for transfers between devices  368 us (21%)
  local copies, waits for them, and re-layouts  342 us (20%)
  starting transfers between devices  23 us (1%)
  other arithmetic  17.8 us (1%)
    dot_general x56, matrix products, product_of(): return jnp.einsum(form, matrix, values, preferred_element_type=jnp.float32)  979 us
    all_to_all x1, waiting for transfers between devices, on_device(): lax.all_to_all(compressed, ('rg', 'az'), split_axis=2, concat_axis=1, til...  368 us
    unnamed x77, local copies, waits for them, and re-layouts  111 us
    another operation x3, local copies, waits for them, and re-layouts, on_device(): jnp.stack(range_compress((raw_pulses[0], raw_pulses[1]), range_phase))  87.8 us
    all_to_all x1, local copies, waits for them, and re-layouts, on_device(): lax.all_to_all(compressed, ('rg', 'az'), split_axis=2, concat_axis=1, til...  50.6 us
  transfers between devices with their start and end apart: 2, of which 1 were waited for; matrix products, arithmetic and copies ran while one was open for 14% of the time, Pallas kernels for 0%

commit v1 on v0

v1 whole, which is shorter than its diff:
```python
import functools
import math

import jax
import jax.numpy as jnp
import numpy as np
from jax import lax
from jax.experimental import pallas as pl
from jax.experimental.pallas import tpu as pltpu
from jax.sharding import PartitionSpec as P

RA = 256
RB = 256
MA = 8
MB = 256
ROWS = 16
CHUNK = 256
LANES = 128
MESH = pl.DeviceIdType.MESH
F32 = jnp.float32
BF16 = jnp.bfloat16
VMEM_LIMIT = 60 * 1024 * 1024


def dft(length, sign):
    grid = np.outer(np.arange(length), np.arange(length)) % length
    angles = sign * 2.0 * np.pi / length * grid
    return np.cos(angles) / math.sqrt(length), np.sin(angles) / math.sqrt(length)


def left_table(length, sign):
    real, imag = dft(length, sign)
    return jnp.asarray(np.block([[real, -imag], [imag, real]]).astype(np.float32), BF16)


def right_table(length, sign):
    real, imag = dft(length, sign)
    return jnp.asarray(np.block([[real, imag], [-imag, real]]).astype(np.float32), BF16)


def twiddle(first, second, sign, scale=1.0):
    grid = np.outer(np.arange(first), np.arange(second)) % (first * second)
    angles = sign * 2.0 * np.pi / (first * second) * grid
    return np.stack([np.cos(angles) * scale, np.sin(angles) * scale]).astype(np.float32)


def dot(a, b):
    return jnp.dot(a, b, preferred_element_type=F32)


def rotated(re, im, cosine, sine):
    return re * cosine - im * sine, re * sine + im * cosine


def pair(re, im, axis):
    return jnp.concatenate([re.astype(BF16), im.astype(BF16)], axis=axis)


def flat_index(naz):
    return lax.axis_index("rg") * naz + lax.axis_index("az")


def coords(flat, naz):
    return (flat // naz, lax.rem(flat, naz))


def greet_all(me, total, naz):
    barrier = pltpu.get_barrier_semaphore()

    def signal(k, carry):
        pl.semaphore_signal(
            barrier, inc=1, device_id=coords(lax.rem(me + k, total), naz), device_id_type=MESH
        )
        return carry

    lax.fori_loop(1, total, signal, 0)
    pl.semaphore_wait(barrier, total - 1)


def range_chain(re, im, fl, fr, gr, gl, wf, wb, middle):
    spec = dot(fl[...], pair(re, im, 0))
    re, im = rotated(spec[:RA], spec[RA:], wf[0], wf[1])
    spec = dot(pair(re, im, 1), fr[...])
    re, im = middle(spec[:, :RB], spec[:, RB:])
    spec = dot(pair(re, im, 1), gr[...])
    re, im = rotated(spec[:, :RB], spec[:, RB:], wb[0], wb[1])
    spec = dot(gl[...], pair(re, im, 0))
    return spec[:RA], spec[RA:]


def compress_kernel(
    total, naz, batches, width, groups,
    raw, phase, fl, fr, gr, gl, wf, wb, rate, afl, agl, awf, awb, squares, turned, mag,
    block, work, ready, x, y, size, load_sem, own_sem, send_sem, recv_sem, x_sem, size_sem,
):
    me = flat_index(naz)
    mine = batches * ROWS
    wide = width // groups

    def load(b, slot):
        return pltpu.make_async_copy(
            raw.at[:, pl.ds(b * ROWS, ROWS), :], block.at[slot], load_sem.at[slot]
        )

    load(0, 0).start()
    greet_all(me, total, naz)

    def send(g, k, start, count):
        peer = lax.rem(me + k, total)
        return pltpu.make_async_remote_copy(
            src_ref=ready.at[:, pl.ds(start, count), pl.ds(peer * width + g * wide, wide)],
            dst_ref=turned.at[:, pl.ds(me * mine + start, count), pl.ds(g * wide, wide)],
            send_sem=send_sem.at[g, k],
            recv_sem=recv_sem.at[g, k],
            device_id=coords(peer, naz),
            device_id_type=MESH,
        )

    def start_group(g, start, count):
        def each(k, carry):
            send(g, k, start, count).start()
            return carry

        lax.fori_loop(1, total, each, 0)

    def own(b):
        return pltpu.make_async_copy(
            ready.at[:, pl.ds(b * ROWS, ROWS), pl.ds(me * width, width)],
            turned.at[:, pl.ds(me * mine + b * ROWS, ROWS), :],
            own_sem.at[b],
        )

    def middle(re, im):
        return rotated(re, im, phase[0], phase[1])

    for b in range(batches):
        slot = b % 2
        if b + 1 < batches:
            load(b + 1, 1 - slot).start()
        load(b, slot).wait()

        def spread(n1, carry):
            for c in range(2):
                piece = block[slot, c, :, pl.ds(pl.multiple_of(n1 * RB, RB), RB)].astype(F32)
                for h in range(2):
                    work[c, h, pl.ds(n1, ROWS, stride=RA), :] = piece[:, h * LANES:(h + 1) * LANES]
            return carry

        lax.fori_loop(0, RA, spread, 0, unroll=4)

        def one_pulse(p, carry):
            rows = pl.ds(pl.multiple_of(p * RA, RA), RA)
            re = jnp.concatenate([work[0, 0, rows, :], work[0, 1, rows, :]], axis=1)
            im = jnp.concatenate([work[1, 0, rows, :], work[1, 1, rows, :]], axis=1)
            res = range_chain(re, im, fl, fr, gr, gl, wf, wb, middle)
            for c in range(2):
                for h in range(2):
                    work[c, h, rows, :] = res[c][:, h * LANES:(h + 1) * LANES]
            return carry

        lax.fori_loop(0, ROWS, one_pulse, 0)

        def gather(n1, carry):
            for c in range(2):
                piece = jnp.concatenate(
                    [work[c, h, pl.ds(n1, ROWS, stride=RA), :] for h in range(2)], axis=1
                )
                ready[c, pl.ds(b * ROWS, ROWS), pl.ds(pl.multiple_of(n1 * RB, RB), RB)] = (
                    piece.astype(BF16)
                )
            return carry

        lax.fori_loop(0, RA, gather, 0, unroll=4)
        start_group(0, b * ROWS, ROWS)
        own(b).start()

    if groups > 1:
        start_group(1, 0, mine)
    for b in range(batches):
        own(b).wait()

    parts = wide // CHUNK

    def column_in(j, slot):
        return pltpu.make_async_copy(
            turned.at[:, :, pl.ds(j * CHUNK, CHUNK)], x.at[slot], x_sem.at[slot]
        )

    def size_out(j):
        return pltpu.make_async_copy(size, mag.at[:, pl.ds(j * CHUNK, CHUNK)], size_sem)

    for g in range(groups):
        def arrive(k, carry):
            send(g, k, 0, mine).wait_recv()
            return carry

        lax.fori_loop(1, total, arrive, 0)
        column_in(g * parts, 0).start()
        if g + 2 < groups:
            start_group(g + 2, 0, mine)
        for part in range(parts):
            j = g * parts + part
            slot = part % 2
            column_in(j, slot).wait()
            if part + 1 < parts:
                column_in(j + 1, 1 - slot).start()
            azimuth_forward(x.at[slot], awf, y)
            azimuth_middle(rate[:, j * CHUNK:(j + 1) * CHUNK], afl, agl, awb, squares, y, work)
            if j > 0:
                size_out(j - 1).wait()
            azimuth_backward(work, size)
            size_out(j).start()
    size_out(groups * parts - 1).wait()

    for g in range(groups):
        def sent(k, carry):
            send(g, k, 0, mine).wait_send()
            return carry

        lax.fori_loop(1, total, sent, 0)


def butterflies(values, sign):
    if len(values) == 1:
        return values
    half = len(values) // 2
    even = butterflies(values[0::2], sign)
    odd = butterflies(values[1::2], sign)
    first, second = [], []
    for k in range(half):
        re, im = odd[k]
        turn = sign * 2.0 * math.pi * k / len(values)
        cosine, sine = math.cos(turn), math.sin(turn)
        if k == 0:
            pass
        elif 4 * k == len(values):
            re, im = (im, -re) if sign < 0 else (-im, re)
        elif abs(abs(cosine) - abs(sine)) < 1e-9:
            size = abs(cosine)
            a = re if cosine > 0 else -re
            b = im if cosine > 0 else -im
            c = re if sine > 0 else -re
            d = im if sine > 0 else -im
            re, im = (a - d) * size, (c + b) * size
        else:
            re, im = re * cosine - im * sine, re * sine + im * cosine
        first.append((even[k][0] + re, even[k][1] + im))
        second.append((even[k][0] - re, even[k][1] - im))
    return first + second


def sincos_fit():
    grid = np.cos(np.linspace(0.0, np.pi, 4001)) * 0.5
    square = grid * grid
    cosine = np.polynomial.chebyshev.Chebyshev.fit(
        square, np.cos(2 * np.pi * grid), 6, domain=[0, 0.25]
    ).convert(kind=np.polynomial.Polynomial).coef
    ratio = np.where(np.abs(grid) < 1e-9, 2 * np.pi, np.sin(2 * np.pi * grid) / np.where(np.abs(grid) < 1e-9, 1.0, grid))
    sine = np.polynomial.chebyshev.Chebyshev.fit(
        square, ratio, 6, domain=[0, 0.25]
    ).convert(kind=np.polynomial.Polynomial).coef
    return [float(x) for x in cosine], [float(x) for x in sine]


def horner(coefs, x):
    value = coefs[-1] * x + coefs[-2]
    for c in coefs[-3::-1]:
        value = value * x + c
    return value


def tile_at(i):
    t, h = i // 2, lax.rem(i, 2)
    return t * ROWS, pl.ds(pl.multiple_of(h * LANES, LANES), LANES)


def rows_at(start):
    return pl.ds(pl.multiple_of(start, ROWS), ROWS)


def azimuth_forward(x, wf, y):
    def one(i, carry):
        top, lanes = tile_at(i)
        values = [
            tuple(x[c, rows_at(m * MB + top), lanes].astype(F32) for c in range(2))
            for m in range(MA)
        ]
        for f, (re, im) in enumerate(butterflies(values, -1.0)):
            re, im = rotated(re, im, wf[0, f, rows_at(top), :], wf[1, f, rows_at(top), :])
            y[f, rows_at(top), lanes] = re.astype(BF16)
            y[f, rows_at(MB + top), lanes] = im.astype(BF16)
        return carry

    lax.fori_loop(0, 2 * (MB // ROWS), one, 0)


def azimuth_middle(rate, fl, gl, wb, squares, y, z):
    cos_fit, sin_fit = sincos_fit()
    turns = rate * (1.0 / (2.0 * math.pi))

    def one(f, carry):
        spec = dot(fl[...], y[f])
        square = jnp.concatenate([squares[f], squares[f]], axis=1)
        turn = turns * square
        turn = turn - jnp.round(turn)
        power = turn * turn
        re, im = rotated(spec[:MB], spec[MB:], horner(cos_fit, power), horner(sin_fit, power) * turn)
        spec = dot(gl[...], pair(re, im, 0))
        cosine = jnp.concatenate([wb[0, f], wb[0, f]], axis=1)
        sine = jnp.concatenate([wb[1, f], wb[1, f]], axis=1)
        rows = pl.ds(pl.multiple_of(f * MB, MB), MB)
        for c, piece in enumerate(rotated(spec[:MB], spec[MB:], cosine, sine)):
            for h in range(2):
                z[c, h, rows, :] = piece[:, h * LANES:(h + 1) * LANES]
        return carry

    lax.fori_loop(0, MA, one, 0)


def azimuth_backward(z, size):
    for h in range(2):
        def one(t, carry):
            top = t * ROWS
            values = [
                tuple(z[c, h, rows_at(f * MB + top), :] for c in range(2)) for f in range(MA)
            ]
            for m, (re, im) in enumerate(butterflies(values, 1.0)):
                size[rows_at(m * MB + top), h * LANES:(h + 1) * LANES] = (
                    jnp.sqrt(re * re + im * im).astype(BF16)
                )
            return carry

        lax.fori_loop(0, MB // ROWS, one, 0)


def edge_kernel(
    total, naz, batches, width,
    mag, kernel_row, weights, fl, fr, gr, gl, wf, wb, edge_az, edge_rg,
    rows_in, work, rows_out, matrix, column, column_out,
    own_sem, column_sem, column_out_sem, rows_sem, send_sem, recv_sem,
):
    me = flat_index(naz)
    mine = batches * ROWS
    greet_all(me, total, naz)

    def send(b, k):
        peer = lax.rem(me + k, total)
        return pltpu.make_async_remote_copy(
            src_ref=mag.at[pl.ds(peer * mine + b * ROWS, ROWS), :],
            dst_ref=rows_in.at[pl.ds(b * ROWS, ROWS), pl.ds(me * width, width)],
            send_sem=send_sem.at[b, k],
            recv_sem=recv_sem.at[b, k],
            device_id=coords(peer, naz),
            device_id_type=MESH,
        )

    def own(b):
        return pltpu.make_async_copy(
            mag.at[pl.ds(me * mine + b * ROWS, ROWS), :],
            rows_in.at[pl.ds(b * ROWS, ROWS), pl.ds(me * width, width)],
            own_sem.at[b],
        )

    def start_batch(b, carry):
        def start(k, inner):
            send(b, k).start()
            return inner

        lax.fori_loop(1, total, start, 0)
        own(b).start()
        return carry

    lax.fori_loop(0, batches, start_batch, 0)

    pulses = MA * MB
    base = jnp.broadcast_to(kernel_row[...], (MB, pulses))
    base = pltpu.roll(base, 0, 1, stride=1, stride_axis=0).astype(BF16)
    for m in range(MA):
        cut = pulses - m * MB
        rolled = base if m == 0 else jnp.concatenate([base[:, cut:], base[:, :cut]], axis=1)
        matrix[m * MB:(m + 1) * MB, :] = rolled

    chunks = width // CHUNK

    def column_in(j, slot):
        return pltpu.make_async_copy(
            mag.at[:, pl.ds(j * CHUNK, CHUNK)], column.at[slot], column_sem.at[slot]
        )

    def column_back(j, slot):
        return pltpu.make_async_copy(
            column_out.at[slot], edge_az.at[:, pl.ds(j * CHUNK, CHUNK)], column_out_sem.at[slot]
        )

    column_in(0, 0).start()
    for j in range(chunks):
        slot = j % 2
        if j + 1 < chunks:
            column_in(j + 1, 1 - slot).start()
        column_in(j, slot).wait()
        if j >= 2:
            column_back(j - 2, slot).wait()

        def part(m, carry):
            rows = pl.ds(pl.multiple_of(m * MB, MB), MB)
            column_out[slot, rows, :] = dot(matrix[rows, :], column[slot])
            return carry

        lax.fori_loop(0, MA, part, 0)
        column_back(j, slot).start()
    for j in range(max(chunks - 2, 0), chunks):
        column_back(j, j % 2).wait()

    def middle(re, im):
        return -weights[...] * im, weights[...] * re

    def rows_back(b, slot):
        return pltpu.make_async_copy(
            rows_out.at[slot], edge_rg.at[pl.ds(b * ROWS, ROWS), :], rows_sem.at[slot]
        )

    for b in range(batches):
        slot = b % 2

        def arrive(k, carry):
            send(b, k).wait_recv()
            return carry

        lax.fori_loop(1, total, arrive, 0)
        own(b).wait()

        def spread(n1, carry):
            piece = rows_in[pl.ds(b * ROWS, ROWS), pl.ds(pl.multiple_of(n1 * RB, RB), RB)].astype(F32)
            for h in range(2):
                work[h, pl.ds(n1, ROWS, stride=RA), :] = piece[:, h * LANES:(h + 1) * LANES]
            return carry

        lax.fori_loop(0, RA, spread, 0, unroll=4)

        def one_pair(q, carry):
            both = [pl.ds(pl.multiple_of((q + o) * RA, RA), RA) for o in (0, ROWS // 2)]
            re, im = (jnp.concatenate([work[0, r, :], work[1, r, :]], axis=1) for r in both)
            res = range_chain(re, im, fl, fr, gr, gl, wf, wb, middle)
            for c in range(2):
                for h in range(2):
                    work[h, both[c], :] = res[c][:, h * LANES:(h + 1) * LANES]
            return carry

        lax.fori_loop(0, ROWS // 2, one_pair, 0)
        if b >= 2:
            rows_back(b - 2, slot).wait()

        def gather(n1, carry):
            piece = jnp.concatenate([work[h, pl.ds(n1, ROWS, stride=RA), :] for h in range(2)], axis=1)
            rows_out[slot, :, pl.ds(pl.multiple_of(n1 * RB, RB), RB)] = piece
            return carry

        lax.fori_loop(0, RA, gather, 0, unroll=4)
        rows_back(b, slot).start()
    for b in range(max(batches - 2, 0), batches):
        rows_back(b, b % 2).wait()

    def sent(b, carry):
        def each(k, inner):
            send(b, k).wait_send()
            return inner

        return lax.fori_loop(1, total, each, carry)

    lax.fori_loop(0, batches, sent, 0)


def lane_table(table):
    return jnp.broadcast_to(jnp.asarray(table)[..., None], table.shape + (LANES,))


def on_device(total, naz, raw_pulses, range_phase, azimuth_rate, conc_azimuth, conc_range):
    mine, bins = raw_pulses.shape[1], raw_pulses.shape[2]
    width = azimuth_rate.shape[0]
    pulses = conc_azimuth.shape[0]
    batches = mine // ROWS
    vmem = pl.BlockSpec(memory_space=pltpu.VMEM)
    hbm = pl.BlockSpec(memory_space=pl.ANY)
    range_tables = (left_table(RA, -1.0), right_table(RB, -1.0), right_table(RB, 1.0), left_table(RA, 1.0))
    range_twiddles = (jnp.asarray(twiddle(RA, RB, -1.0)), jnp.asarray(twiddle(RA, RB, 1.0)))

    with jax.named_scope("compress"):
        groups = max(1, min(4, width // CHUNK))
        grid = range_phase.reshape(RB, RA).T
        phase = jnp.stack([jnp.cos(grid), jnp.sin(grid)])
        scale = 1.0 / math.sqrt(MA)
        freqs = np.arange(MA)[:, None] + MA * np.arange(MB)[None, :]
        signed = np.where(freqs < pulses // 2, freqs, freqs - pulses) / pulses
        squares = lane_table((signed * signed).astype(np.float32))
        _, magnitude = pl.pallas_call(
            functools.partial(compress_kernel, total, naz, batches, width, groups),
            out_shape=(
                jax.ShapeDtypeStruct((2, pulses, width), BF16),
                jax.ShapeDtypeStruct((pulses, width), BF16),
            ),
            in_specs=[hbm] + [vmem] * 13,
            out_specs=(hbm, hbm),
            scratch_shapes=[
                pltpu.VMEM((2, 2, ROWS, bins), BF16),
                pltpu.VMEM((2, 2, ROWS * RA, LANES), F32),
                pltpu.VMEM((2, mine, bins), BF16),
                pltpu.VMEM((2, 2, pulses, CHUNK), BF16),
                pltpu.VMEM((MA, 2 * MB, CHUNK), BF16),
                pltpu.VMEM((pulses, CHUNK), BF16),
                pltpu.SemaphoreType.DMA((2,)),
                pltpu.SemaphoreType.DMA((batches,)),
                pltpu.SemaphoreType.DMA((groups, total)),
                pltpu.SemaphoreType.DMA((groups, total)),
                pltpu.SemaphoreType.DMA((2,)),
                pltpu.SemaphoreType.DMA,
            ],
            compiler_params=pltpu.CompilerParams(
                collective_id=0, has_side_effects=True, vmem_limit_bytes=VMEM_LIMIT
            ),
            name="compress",
        )(
            raw_pulses, phase, *range_tables, *range_twiddles,
            azimuth_rate.reshape(1, width), left_table(MB, -1.0), left_table(MB, 1.0),
            lane_table(twiddle(MA, MB, -1.0, scale)), lane_table(twiddle(MA, MB, 1.0, scale)), squares,
        )

    with jax.named_scope("edge_maps"):
        half = pulses // 2
        mixed = conc_azimuth[1:half] + conc_azimuth[:half:-1]
        index = np.arange(1, half)
        sines = np.sin(2.0 * np.pi / pulses * (np.outer(index, index) % pulses)) / pulses
        taps = jnp.sum(jnp.asarray(sines.astype(np.float32)) * mixed[None, :], axis=1)
        zero = jnp.zeros((1,), F32)
        kernel_row = jnp.concatenate([zero, taps, zero, -taps[::-1]]).reshape(1, pulses)
        mirrored = jnp.concatenate([conc_range[:1], conc_range[:0:-1]])
        place = jnp.arange(bins, dtype=jnp.int32)
        signs = jnp.where(place < bins // 2, 1.0, -1.0) * ((place != 0) & (place != bins // 2))
        weights = (0.5 * signs * (conc_range + mirrored)).reshape(RB, RA).T
        return pl.pallas_call(
            functools.partial(edge_kernel, total, naz, batches, width),
            out_shape=(
                jax.ShapeDtypeStruct((pulses, width), F32),
                jax.ShapeDtypeStruct((mine, bins), F32),
            ),
            in_specs=[hbm] + [vmem] * 8,
            out_specs=(hbm, hbm),
            scratch_shapes=[
                pltpu.VMEM((mine, bins), BF16),
                pltpu.VMEM((2, ROWS * RA, LANES), F32),
                pltpu.VMEM((2, ROWS, bins), F32),
                pltpu.VMEM((pulses, pulses), BF16),
                pltpu.VMEM((2, pulses, CHUNK), BF16),
                pltpu.VMEM((2, pulses, CHUNK), F32),
                pltpu.SemaphoreType.DMA((batches,)),
                pltpu.SemaphoreType.DMA((2,)),
                pltpu.SemaphoreType.DMA((2,)),
                pltpu.SemaphoreType.DMA((2,)),
                pltpu.SemaphoreType.DMA((batches, total)),
                pltpu.SemaphoreType.DMA((batches, total)),
            ],
            compiler_params=pltpu.CompilerParams(
                collective_id=1, has_side_effects=True, vmem_limit_bytes=VMEM_LIMIT
            ),
            name="edge_maps",
        )(magnitude, kernel_row, weights, *range_tables, *range_twiddles)


def solution(mesh):
    total = mesh.shape["rg"] * mesh.shape["az"]
    in_specs = (P(None, ("rg", "az"), None), P(), P(("rg", "az")), P(), P())
    out_specs = (P(None, ("rg", "az")), P(("rg", "az"), None))
    return jax.shard_map(
        functools.partial(on_device, total, mesh.shape["az"]),
        mesh=mesh, in_specs=in_specs, out_specs=out_specs, check_vma=False,
    )
```

time: 1750 us -> 730 us (0.42)
  matrix products: 979 us -> 0 us
  Pallas kernels: 0 us -> 685 us
  waiting for transfers between devices: 368 us -> 0 us
  local copies, waits for them, and re-layouts: 342 us -> 35.3 us
  starting transfers between devices: 23 us -> 0 us
    dot_general x56 -> x0, matrix products: 979 us -> none  [product_of(): return jnp.einsum(form, matrix, values, preferred_element_type=jnp.float32)]
    pallas_call x0 -> x2, Pallas kernels: none -> 685 us  [the longest x1 472 us: on_device(): pl.pallas_call(functools.partial(compress_kernel, total, naz, batches, wi...]
    all_to_all x2 -> x0, waiting for transfers between devices: 368 us -> none  [the longest x1 368 us: on_device(): lax.all_to_all(compressed, ('rg', 'az'), split_axis=2, concat_axis=1, til...]
    another operation x3 -> x0, local copies, waits for them, and re-layouts: 87.8 us -> none  [on_device(): jnp.stack(range_compress((raw_pulses[0], raw_pulses[1]), range_phase))]
    unnamed x77 -> x14, local copies, waits for them, and re-layouts: 111 us -> 23.3 us
    all_to_all x2 -> x0, local copies, waits for them, and re-layouts: 62 us -> none  [the longest x1 50.6 us: on_device(): lax.all_to_all(compressed, ('rg', 'az'), split_axis=2, concat_axis=1, til...]
    convert_element_type x3 -> x0, local copies, waits for them, and re-layouts: 35.1 us -> none  [the longest x2 23.8 us: range_compress(): piece.astype(jnp.bfloat16).reshape(count, RA * RB)]
    all_to_all x2 -> x0, starting transfers between devices: 23 us -> none  [the longest x1 15.6 us: on_device(): lax.all_to_all(magnitude, ('rg', 'az'), split_axis=0, concat_axis=1, tile...]
  transfers between devices with their start and end apart: 2 -> 0, of which waited for: 1 -> 0; matrix products, arithmetic and copies ran while one was open for 14% -> 0% of each run, Pallas kernels for 0% -> 0%
where the time goes in v1:
time: 730 us; the launch traced here: 727 us
  Pallas kernels  685 us (94%)
  local copies, waits for them, and re-layouts  35.3 us (5%)
    pallas_call x1, Pallas kernels, on_device(): pl.pallas_call(functools.partial(compress_kernel, total, naz, batches, wi...  472 us
    pallas_call x1, Pallas kernels, on_device(): pl.pallas_call(functools.partial(edge_kernel, total, naz, batches, width)...  213 us
    unnamed x14, local copies, waits for them, and re-layouts  23.3 us

profile of v1, /device:TPU:0, one launch (start us, length us, event | category | flops | bytes accessed | tf_op | source)
XLA Modules:
  0.0 727.1 jit_solution(10528545821119085109)
XLA Ops:
  0.7 1.2 slice.14
  1.9 0.8 slice.13
  2.6 0.1 reverse
  2.7 0.8 slice_add_fusion
  3.5 2.6 multiply_reduce_fusion
  6.0 0.1 reverse.1
  6.2 0.7 concatenate.6
  6.9 1.1 slice.15
  7.9 0.4 reverse.2
  8.3 0.1 slice.19
  8.4 1.7 fusion
  10.3 0.8 copy.24
  11.1 1.9 fusion.2
  13.1 0.1 copy.22
  13.3 0.1 copy.23
  13.4 0.8 pad_maximum_fusion.phase
  14.3 1.3 broadcast_in_dim.14.squares
  15.6 1.9 broadcast_in_dim.12.awf
  17.5 1.9 broadcast_in_dim.13.awb
  19.4 471.8 %compress.1 = (bf16[2,2048,2048]{2,1,0:T(8,128)(2,1)}, bf16[2048,2048]{1,0:T(8,128)(2,1)}) custom-call(bf16[2,64,65536]{2,1,0:T(8,128)(2,1)} %raw.1, f32[2,256,256]{2,1,0:T(8,128)} %pad_maximum_fusion.phase, bf16[512,512]{1,0:T(8,128)(2,1)} %constant.31.clone.fl.gr.afl, bf16[512,512]{1,0:T(8,128)(2,1)} %constant.32.clone.fr.gl.agl, ...), custom_call_target="tpu_custom_call" | custom-call | tf_op jit(solution)/shard_map/compress/compress/pallas_call | solution.py:495
  491.2 213.3 %edge_maps.1 = (f32[2048,2048]{1,0:T(8,128)}, f32[64,65536]{1,0:T(8,128)}) custom-call(bf16[2048,2048]{1,0:T(8,128)(2,1)} %get-tuple-element.3.mag, f32[1,2048]{1,0:T(1,128)} %bitcast.17, f32[256,256]{1,0:T(8,128)} %bitcast.12, bf16[512,512]{1,0:T(8,128)(2,1)} %constant.31.clone.fl.gr.afl, bf16[512,512]{1,0:T(8,128)(2,1)} %constant.32.clone.fr.gl.agl, ...), custom_call_target="tpu_custom_call" | custom-call | tf_op jit(solution)/shard_map/edge_maps/edge_maps/pallas_call | solution.py:539
  704.5 12.7 %copy.27 = f32[2048,2048]{1,0:T(8,128)} copy(f32[2048,2048]{1,0:T(8,128)} %get-tuple-element.8) | data formatting | bytes 33554432
  717.2 3.7 copy-done
  721.0 6.2 copy.28
  (11 shorter events, 0.3 us)
Async XLA Ops:
  0.6 13.6 %copy-start.3 = (f32[8,256]{1,0:T(8,128)S(1)}, f32[8,256]{1,0:T(8,128)}, u32[]{:S(2)}) copy-start(f32[8,256]{1,0:T(8,128)} %constant.35.clone) | copy-start | bytes 24580
  0.6 14.9 %copy-start.2 = (f32[2,8,256]{2,1,0:T(8,128)S(1)}, f32[2,8,256]{2,1,0:T(8,128)}, u32[]{:S(2)}) copy-start(f32[2,8,256]{2,1,0:T(8,128)} %constant.36.clone) | copy-start | bytes 49156
  0.7 16.8 %copy-start.1 = (f32[2,8,256]{2,1,0:T(8,128)S(1)}, f32[2,8,256]{2,1,0:T(8,128)}, u32[]{:S(2)}) copy-start(f32[2,8,256]{2,1,0:T(8,128)} %constant.37.clone) | copy-start | bytes 49156
  704.5 16.4 %copy-start = (f32[64,65536]{1,0:T(8,128)S(1)}, f32[64,65536]{1,0:T(8,128)}, u32[]{:S(2)}) copy-start(f32[64,65536]{1,0:T(8,128)} %get-tuple-element.9) | copy-start | bytes 50331652

commit v2 on v1

v2 whole, which is shorter than its diff:
```python
import functools
import math

import jax
import jax.numpy as jnp
import numpy as np
from jax import lax
from jax.experimental import pallas as pl
from jax.experimental.pallas import tpu as pltpu
from jax.sharding import PartitionSpec as P

RA = 256
RB = 256
MA = 8
MB = 256
ROWS = 16
CHUNK = 256
LANES = 128
MESH = pl.DeviceIdType.MESH
F32 = jnp.float32
BF16 = jnp.bfloat16
VMEM_LIMIT = 60 * 1024 * 1024


def dft(length, sign):
    grid = np.outer(np.arange(length), np.arange(length)) % length
    angles = sign * 2.0 * np.pi / length * grid
    return np.cos(angles) / math.sqrt(length), np.sin(angles) / math.sqrt(length)


def left_table(length, sign):
    real, imag = dft(length, sign)
    return jnp.asarray(np.block([[real, -imag], [imag, real]]).astype(np.float32), BF16)


def right_table(length, sign):
    real, imag = dft(length, sign)
    return jnp.asarray(np.block([[real, imag], [-imag, real]]).astype(np.float32), BF16)


def twiddle(first, second, sign, scale=1.0):
    grid = np.outer(np.arange(first), np.arange(second)) % (first * second)
    angles = sign * 2.0 * np.pi / (first * second) * grid
    return np.stack([np.cos(angles) * scale, np.sin(angles) * scale]).astype(np.float32)


def dot(a, b):
    return jnp.dot(a, b, preferred_element_type=F32)


def rotated(re, im, cosine, sine):
    return re * cosine - im * sine, re * sine + im * cosine


def pair(re, im, axis):
    return jnp.concatenate([re.astype(BF16), im.astype(BF16)], axis=axis)


def flat_index(naz):
    return lax.axis_index("rg") * naz + lax.axis_index("az")


def coords(flat, naz):
    return (flat // naz, lax.rem(flat, naz))


def greet_all(me, total, naz):
    barrier = pltpu.get_barrier_semaphore()

    def signal(k, carry):
        pl.semaphore_signal(
            barrier, inc=1, device_id=coords(lax.rem(me + k, total), naz), device_id_type=MESH
        )
        return carry

    lax.fori_loop(1, total, signal, 0)
    pl.semaphore_wait(barrier, total - 1)


def range_chain(re, im, fl, fr, gr, gl, wf, wb, middle):
    spec = dot(fl[...], pair(re, im, 0))
    re, im = rotated(spec[:RA], spec[RA:], wf[0], wf[1])
    spec = dot(pair(re, im, 1), fr[...])
    re, im = middle(spec[:, :RB], spec[:, RB:])
    spec = dot(pair(re, im, 1), gr[...])
    re, im = rotated(spec[:, :RB], spec[:, RB:], wb[0], wb[1])
    spec = dot(gl[...], pair(re, im, 0))
    return spec[:RA], spec[RA:]


def image_kernel(
    total, naz, batches, width, groups,
    raw, phase, fl, fr, gr, gl, wf, wb, rate, awf, awb, squares, kernel_row, weights,
    turned, mag, rows_in, edge_az, edge_rg,
    block, work, ready, x, y, size, base, column_out, rows_out,
    load_sem, own_sem, send_sem, recv_sem, x_sem, size_sem, column_sem, rows_sem,
    early_send, early_recv, late_send, late_recv,
):
    me = flat_index(naz)
    mine = batches * ROWS
    wide = width // groups
    pulses = MA * MB
    eager = min(2, groups)

    def load(b, slot):
        return pltpu.make_async_copy(
            raw.at[:, pl.ds(b * ROWS, ROWS), :], block.at[slot], load_sem.at[slot]
        )

    load(0, 0).start()
    greet_all(me, total, naz)

    def over_peers(act):
        def each(k, carry):
            act(k)
            return carry

        lax.fori_loop(1, total, each, 0)

    def send(g, k, start, count):
        peer = lax.rem(me + k, total)
        return pltpu.make_async_remote_copy(
            src_ref=ready.at[:, pl.ds(start, count), pl.ds(peer * width + g * wide, wide)],
            dst_ref=turned.at[:, pl.ds(me * mine + start, count), pl.ds(g * wide, wide)],
            send_sem=send_sem.at[g, k],
            recv_sem=recv_sem.at[g, k],
            device_id=coords(peer, naz),
            device_id_type=MESH,
        )

    def own(b):
        return pltpu.make_async_copy(
            ready.at[:, pl.ds(b * ROWS, ROWS), pl.ds(me * width, width)],
            turned.at[:, pl.ds(me * mine + b * ROWS, ROWS), :],
            own_sem.at[b],
        )

    def middle(re, im):
        return rotated(re, im, phase[0], phase[1])

    for b in range(batches):
        slot = b % 2
        if b + 1 < batches:
            load(b + 1, 1 - slot).start()
        load(b, slot).wait()

        def spread(n1, carry):
            for c in range(2):
                piece = block[slot, c, :, pl.ds(pl.multiple_of(n1 * RB, RB), RB)].astype(F32)
                for h in range(2):
                    work[c, h, pl.ds(n1, ROWS, stride=RA), :] = piece[:, h * LANES:(h + 1) * LANES]
            return carry

        lax.fori_loop(0, RA, spread, 0, unroll=4)

        def one_pulse(p, carry):
            rows = pl.ds(pl.multiple_of(p * RA, RA), RA)
            re = jnp.concatenate([work[0, 0, rows, :], work[0, 1, rows, :]], axis=1)
            im = jnp.concatenate([work[1, 0, rows, :], work[1, 1, rows, :]], axis=1)
            res = range_chain(re, im, fl, fr, gr, gl, wf, wb, middle)
            for c in range(2):
                for h in range(2):
                    work[c, h, rows, :] = res[c][:, h * LANES:(h + 1) * LANES]
            return carry

        lax.fori_loop(0, ROWS, one_pulse, 0, unroll=2)

        def gather(n1, carry):
            for c in range(2):
                piece = jnp.concatenate(
                    [work[c, h, pl.ds(n1, ROWS, stride=RA), :] for h in range(2)], axis=1
                )
                ready[c, pl.ds(b * ROWS, ROWS), pl.ds(pl.multiple_of(n1 * RB, RB), RB)] = (
                    piece.astype(BF16)
                )
            return carry

        lax.fori_loop(0, RA, gather, 0, unroll=4)
        for g in range(eager):
            over_peers(lambda k: send(g, k, b * ROWS, ROWS).start())
        own(b).start()

    taps = jnp.broadcast_to(kernel_row[...], (MB, pulses))
    base[...] = pltpu.roll(taps, 0, 1, stride=1, stride_axis=0).astype(BF16)
    for b in range(batches):
        own(b).wait()

    parts = wide // CHUNK
    early = (groups - 1) * wide

    def column_in(j, slot):
        return pltpu.make_async_copy(
            turned.at[:, :, pl.ds(j * CHUNK, CHUNK)], x.at[slot], x_sem.at[slot]
        )

    def size_out(j):
        return pltpu.make_async_copy(
            size.at[pl.ds(0, pulses), :], mag.at[:, pl.ds(j * CHUNK, CHUNK)], size_sem
        )

    def column_back(j):
        return pltpu.make_async_copy(
            column_out, edge_az.at[:, pl.ds(j * CHUNK, CHUNK)], column_sem
        )

    def send_back(k, row, rows, column, columns, sent_sem, here_sem):
        peer = lax.rem(me + k, total)
        return pltpu.make_async_remote_copy(
            src_ref=mag.at[pl.ds(peer * mine + row, rows), pl.ds(column, columns)],
            dst_ref=rows_in.at[pl.ds(row, rows), pl.ds(me * width + column, columns)],
            send_sem=sent_sem,
            recv_sem=here_sem,
            device_id=coords(peer, naz),
            device_id_type=MESH,
        )

    def send_early(k, column, columns):
        return send_back(k, 0, mine, column, columns, early_send.at[k], early_recv.at[k])

    def send_late(k, b):
        return send_back(
            k, b * ROWS, ROWS, early, wide, late_send.at[b, k], late_recv.at[b, k]
        )

    for g in range(groups):
        over_peers(lambda k: send(g, k, 0, mine).wait_recv())
        column_in(g * parts, 0).start()
        if g + eager < groups:
            over_peers(lambda k: send(g + eager, k, 0, mine).start())
        for part in range(parts):
            j = g * parts + part
            slot = part % 2
            column_in(j, slot).wait()
            if part + 1 < parts:
                column_in(j + 1, 1 - slot).start()
            azimuth_forward(x.at[slot], awf, y)
            azimuth_middle(rate[:, j * CHUNK:(j + 1) * CHUNK], fl, gl, awb, squares, y, work)
            azimuth_backward(work, size)
            size_out(j).start()
            if part + 1 == parts:
                size_out(j).wait()
                if g + 1 < groups:
                    over_peers(lambda k: send_early(k, g * wide, wide).start())
                else:
                    for b in range(min(2, batches)):
                        over_peers(lambda k: send_late(k, b).start())
            if j > 0:
                column_back(j - 1).wait()

            def edges(m, carry):
                rows = pl.ds(pl.multiple_of(m * MB, MB), MB)
                column_out[rows, :] = dot(base[...], size[pl.ds(pl.multiple_of(m * MB, MB), pulses), :])
                return carry

            lax.fori_loop(0, MA, edges, 0)
            column_back(j).start()
            if part + 1 < parts:
                size_out(j).wait()
    own_rows = pltpu.make_async_copy(
        mag.at[pl.ds(me * mine, mine), :], rows_in.at[:, pl.ds(me * width, width)], size_sem
    )
    own_rows.start()
    own_rows.wait()
    column_back(groups * parts - 1).wait()
    if early:
        over_peers(lambda k: send_early(k, 0, early).wait_recv())

    def turn(re, im):
        return -weights[...] * im, weights[...] * re

    def rows_load(b):
        return pltpu.make_async_copy(
            rows_in.at[pl.ds(b * ROWS, ROWS), :], block.at[0, 0], load_sem.at[0]
        )

    def rows_back(b):
        return pltpu.make_async_copy(rows_out, edge_rg.at[pl.ds(b * ROWS, ROWS), :], rows_sem)

    for b in range(batches):
        over_peers(lambda k: send_late(k, b).wait_recv())
        if b + 2 < batches:
            over_peers(lambda k: send_late(k, b + 2).start())
        rows_load(b).start()
        rows_load(b).wait()

        def spread_rows(n1, carry):
            piece = block[0, 0, :, pl.ds(pl.multiple_of(n1 * RB, RB), RB)].astype(F32)
            for h in range(2):
                work[0, h, pl.ds(n1, ROWS, stride=RA), :] = piece[:, h * LANES:(h + 1) * LANES]
            return carry

        lax.fori_loop(0, RA, spread_rows, 0, unroll=4)

        def one_pair(q, carry):
            both = [pl.ds(pl.multiple_of((q + o) * RA, RA), RA) for o in (0, ROWS // 2)]
            re, im = (jnp.concatenate([work[0, 0, r, :], work[0, 1, r, :]], axis=1) for r in both)
            res = range_chain(re, im, fl, fr, gr, gl, wf, wb, turn)
            for c in range(2):
                for h in range(2):
                    work[0, h, both[c], :] = res[c][:, h * LANES:(h + 1) * LANES]
            return carry

        lax.fori_loop(0, ROWS // 2, one_pair, 0, unroll=2)
        if b > 0:
            rows_back(b - 1).wait()

        def gather_rows(n1, carry):
            piece = jnp.concatenate(
                [work[0, h, pl.ds(n1, ROWS, stride=RA), :] for h in range(2)], axis=1
            )
            rows_out[:, pl.ds(pl.multiple_of(n1 * RB, RB), RB)] = piece
            return carry

        lax.fori_loop(0, RA, gather_rows, 0, unroll=4)
        rows_back(b).start()
    rows_back(batches - 1).wait()

    for g in range(groups):
        over_peers(lambda k: send(g, k, 0, mine).wait_send())
    if early:
        over_peers(lambda k: send_early(k, 0, early).wait_send())
    for b in range(batches):
        over_peers(lambda k: send_late(k, b).wait_send())


def butterflies(values, sign):
    if len(values) == 1:
        return values
    half = len(values) // 2
    even = butterflies(values[0::2], sign)
    odd = butterflies(values[1::2], sign)
    first, second = [], []
    for k in range(half):
        re, im = odd[k]
        turn = sign * 2.0 * math.pi * k / len(values)
        cosine, sine = math.cos(turn), math.sin(turn)
        if k == 0:
            pass
        elif 4 * k == len(values):
            re, im = (im, -re) if sign < 0 else (-im, re)
        elif abs(abs(cosine) - abs(sine)) < 1e-9:
            size = abs(cosine)
            a = re if cosine > 0 else -re
            b = im if cosine > 0 else -im
            c = re if sine > 0 else -re
            d = im if sine > 0 else -im
            re, im = (a - d) * size, (c + b) * size
        else:
            re, im = re * cosine - im * sine, re * sine + im * cosine
        first.append((even[k][0] + re, even[k][1] + im))
        second.append((even[k][0] - re, even[k][1] - im))
    return first + second


def sincos_fit():
    grid = np.cos(np.linspace(0.0, np.pi, 4001)) * 0.5
    square = grid * grid
    cosine = np.polynomial.chebyshev.Chebyshev.fit(
        square, np.cos(2 * np.pi * grid), 6, domain=[0, 0.25]
    ).convert(kind=np.polynomial.Polynomial).coef
    ratio = np.where(np.abs(grid) < 1e-9, 2 * np.pi, np.sin(2 * np.pi * grid) / np.where(np.abs(grid) < 1e-9, 1.0, grid))
    sine = np.polynomial.chebyshev.Chebyshev.fit(
        square, ratio, 6, domain=[0, 0.25]
    ).convert(kind=np.polynomial.Polynomial).coef
    return [float(x) for x in cosine], [float(x) for x in sine]


def horner(coefs, x):
    value = coefs[-1] * x + coefs[-2]
    for c in coefs[-3::-1]:
        value = value * x + c
    return value


def tile_at(i):
    t, h = i // 2, lax.rem(i, 2)
    return t * ROWS, pl.ds(pl.multiple_of(h * LANES, LANES), LANES)


def rows_at(start):
    return pl.ds(pl.multiple_of(start, ROWS), ROWS)


def azimuth_forward(x, wf, y):
    def one(i, carry):
        top, lanes = tile_at(i)
        values = [
            tuple(x[c, rows_at(m * MB + top), lanes].astype(F32) for c in range(2))
            for m in range(MA)
        ]
        for f, (re, im) in enumerate(butterflies(values, -1.0)):
            re, im = rotated(re, im, wf[0, f, rows_at(top), :], wf[1, f, rows_at(top), :])
            y[f, rows_at(top), lanes] = re.astype(BF16)
            y[f, rows_at(MB + top), lanes] = im.astype(BF16)
        return carry

    lax.fori_loop(0, 2 * (MB // ROWS), one, 0)


def azimuth_middle(rate, fl, gl, wb, squares, y, z):
    cos_fit, sin_fit = sincos_fit()
    turns = rate * (1.0 / (2.0 * math.pi))

    def one(f, carry):
        spec = dot(fl[...], y[f])
        square = jnp.concatenate([squares[f], squares[f]], axis=1)
        turn = turns * square
        turn = turn - jnp.round(turn)
        power = turn * turn
        re, im = rotated(spec[:MB], spec[MB:], horner(cos_fit, power), horner(sin_fit, power) * turn)
        spec = dot(gl[...], pair(re, im, 0))
        cosine = jnp.concatenate([wb[0, f], wb[0, f]], axis=1)
        sine = jnp.concatenate([wb[1, f], wb[1, f]], axis=1)
        rows = pl.ds(pl.multiple_of(f * MB, MB), MB)
        for c, piece in enumerate(rotated(spec[:MB], spec[MB:], cosine, sine)):
            for h in range(2):
                z[c, h, rows, :] = piece[:, h * LANES:(h + 1) * LANES]
        return carry

    lax.fori_loop(0, MA, one, 0)


def azimuth_backward(z, size):
    for h in range(2):
        def one(t, carry):
            top = t * ROWS
            values = [
                tuple(z[c, h, rows_at(f * MB + top), :] for c in range(2)) for f in range(MA)
            ]
            for m, (re, im) in enumerate(butterflies(values, 1.0)):
                value = jnp.sqrt(re * re + im * im).astype(BF16)
                for copy in range(2):
                    rows = rows_at((copy * MA + m) * MB + top)
                    size[rows, h * LANES:(h + 1) * LANES] = value
            return carry

        lax.fori_loop(0, MB // ROWS, one, 0)


def lane_table(table):
    return jnp.asarray(np.repeat(table[..., None], LANES, axis=-1))


def on_device(total, naz, raw_pulses, range_phase, azimuth_rate, conc_azimuth, conc_range):
    mine, bins = raw_pulses.shape[1], raw_pulses.shape[2]
    width = azimuth_rate.shape[0]
    pulses = conc_azimuth.shape[0]
    batches = mine // ROWS
    vmem = pl.BlockSpec(memory_space=pltpu.VMEM)
    hbm = pl.BlockSpec(memory_space=pl.ANY)
    range_tables = (left_table(RA, -1.0), right_table(RB, -1.0), right_table(RB, 1.0), left_table(RA, 1.0))
    range_twiddles = (jnp.asarray(twiddle(RA, RB, -1.0)), jnp.asarray(twiddle(RA, RB, 1.0)))

    with jax.named_scope("tables"):
        groups = max(1, min(4, width // CHUNK))
        grid = range_phase.reshape(RB, RA).T
        phase = jnp.stack([jnp.cos(grid), jnp.sin(grid)])
        scale = 1.0 / math.sqrt(MA)
        freqs = np.arange(MA)[:, None] + MA * np.arange(MB)[None, :]
        signed = np.where(freqs < pulses // 2, freqs, freqs - pulses) / pulses
        squares = lane_table((signed * signed).astype(np.float32))
        half = pulses // 2
        mixed = conc_azimuth[1:half] + conc_azimuth[:half:-1]
        index = np.arange(1, half)
        sines = np.sin(2.0 * np.pi / pulses * (np.outer(index, index) % pulses)) / pulses
        taps = jnp.sum(jnp.asarray(sines.astype(np.float32)) * mixed[None, :], axis=1)
        zero = jnp.zeros((1,), F32)
        kernel_row = jnp.concatenate([zero, taps, zero, -taps[::-1]]).reshape(1, pulses)
        mirrored = jnp.concatenate([conc_range[:1], conc_range[:0:-1]])
        place = jnp.arange(bins, dtype=jnp.int32)
        signs = jnp.where(place < bins // 2, 1.0, -1.0) * ((place != 0) & (place != bins // 2))
        weights = (0.5 * signs * (conc_range + mirrored)).reshape(RB, RA).T

    with jax.named_scope("image"):
        dma = pltpu.SemaphoreType.DMA
        _, _, _, edge_azimuth, edge_range = pl.pallas_call(
            functools.partial(image_kernel, total, naz, batches, width, groups),
            out_shape=(
                jax.ShapeDtypeStruct((2, pulses, width), BF16),
                jax.ShapeDtypeStruct((pulses, width), BF16),
                jax.ShapeDtypeStruct((mine, bins), BF16),
                jax.ShapeDtypeStruct((pulses, width), F32),
                jax.ShapeDtypeStruct((mine, bins), F32),
            ),
            in_specs=[hbm] + [vmem] * 13,
            out_specs=(hbm,) * 5,
            scratch_shapes=[
                pltpu.VMEM((2, 2, ROWS, bins), BF16),
                pltpu.VMEM((2, 2, ROWS * RA, LANES), F32),
                pltpu.VMEM((2, mine, bins), BF16),
                pltpu.VMEM((2, 2, pulses, CHUNK), BF16),
                pltpu.VMEM((MA, 2 * MB, CHUNK), BF16),
                pltpu.VMEM((2 * pulses, CHUNK), BF16),
                pltpu.VMEM((MB, pulses), BF16),
                pltpu.VMEM((pulses, CHUNK), F32),
                pltpu.VMEM((ROWS, bins), F32),
                dma((2,)), dma((batches,)), dma((groups, total)), dma((groups, total)),
                dma((2,)), dma, dma, dma,
                dma((total,)), dma((total,)), dma((batches, total)), dma((batches, total)),
            ],
            compiler_params=pltpu.CompilerParams(
                collective_id=0, has_side_effects=True, vmem_limit_bytes=VMEM_LIMIT
            ),
            name="image",
        )(
            raw_pulses, phase, *range_tables, *range_twiddles, azimuth_rate.reshape(1, width),
            lane_table(twiddle(MA, MB, -1.0, scale)), lane_table(twiddle(MA, MB, 1.0, scale)),
            squares, kernel_row, weights,
        )
    return edge_azimuth, edge_range


def solution(mesh):
    total = mesh.shape["rg"] * mesh.shape["az"]
    in_specs = (P(None, ("rg", "az"), None), P(), P(("rg", "az")), P(), P())
    out_specs = (P(None, ("rg", "az")), P(("rg", "az"), None))
    return jax.shard_map(
        functools.partial(on_device, total, mesh.shape["az"]),
        mesh=mesh, in_specs=in_specs, out_specs=out_specs, check_vma=False,
    )
```

time: 730 us -> 685 us (0.938)
  Pallas kernels: 685 us -> 648 us
    pallas_call x2 -> x1, Pallas kernels: 685 us -> 648 us  [on_device(): pl.pallas_call(functools.partial(image_kernel, total, naz, batches, width...]
    unnamed x14 -> x8, local copies, waits for them, and re-layouts: 23.3 us -> 23.2 us
where the time goes in v2:
time: 685 us
  Pallas kernels  648 us (95%)
  local copies, waits for them, and re-layouts  30.1 us (4%)
    pallas_call x1, Pallas kernels, on_device(): pl.pallas_call(functools.partial(image_kernel, total, naz, batches, width...  648 us
    unnamed x8, local copies, waits for them, and re-layouts  23.2 us

profile of v2, /device:TPU:0, one launch (start us, length us, event | category | flops | bytes accessed | tf_op | source)
XLA Modules:
  0.0 684.8 jit_solution(13729187583878134544)
XLA Ops:
  0.6 1.2 slice.14
  1.8 0.8 slice.13
  2.6 0.1 reverse
  2.7 0.8 slice_add_fusion
  3.4 2.6 multiply_reduce_fusion
  6.0 0.1 reverse.1
  6.1 0.1 slice_negate_fusion
  6.1 0.7 concatenate.6
  6.8 1.1 slice.15
  7.9 0.4 reverse.2
  8.2 0.1 slice.19
  8.4 1.7 fusion
  10.1 0.1 reshape.19
  10.2 0.8 copy.22
  11.1 1.9 fusion.2
  12.9 0.1 cos.10
  13.0 0.1 copy.20
  13.1 0.1 sin.10
  13.2 0.1 copy.21
  13.4 0.8 pad_maximum_fusion.phase
  14.2 648.1 %image.1 = (bf16[2,2048,2048]{2,1,0:T(8,128)(2,1)}, bf16[2048,2048]{1,0:T(8,128)(2,1)}, bf16[64,65536]{1,0:T(8,128)(2,1)}, f32[2048,2048]{1,0:T(8,128)}, f32[64,65536]{1,0:T(8,128)}) custom-call(bf16[2,64,65536]{2,1,0:T(8,128)(2,1)} %raw.1, f32[2,256,256]{2,1,0:T(8,128)} %pad_maximum_fusion.phase, bf16[512,512]{1,0:T(8,128)(2,1)} %constant.31.clone.fl.gr, ...), custom_call_target="tpu_custom_call" | custom-call | tf_op jit(solution)/shard_map/image/image/pallas_call | solution.py:476
  662.3 12.7 %copy.25 = f32[2048,2048]{1,0:T(8,128)} copy(f32[2048,2048]{1,0:T(8,128)} %get-tuple-element.10) | data formatting | bytes 33554432
  674.9 3.7 copy-done
  678.7 6.2 copy.26
  (1 shorter events, 0.0 us)
Async XLA Ops:
  662.3 16.4 %copy-start = (f32[64,65536]{1,0:T(8,128)S(1)}, f32[64,65536]{1,0:T(8,128)}, u32[]{:S(2)}) copy-start(f32[64,65536]{1,0:T(8,128)} %get-tuple-element.11) | copy-start | bytes 50331652

commit v3 on v2

--- a/solution.py
+++ b/solution.py
@@ -94,7 +94,7 @@
     turned, mag, rows_in, edge_az, edge_rg,
     block, work, ready, x, y, size, base, column_out, rows_out,
     load_sem, own_sem, send_sem, recv_sem, x_sem, size_sem, column_sem, rows_sem,
-    early_send, early_recv, late_send, late_recv,
+    back_send, back_recv,
 ):
     me = flat_index(naz)
     mine = batches * ROWS
@@ -180,6 +180,8 @@
             over_peers(lambda k: send(g, k, b * ROWS, ROWS).start())
         own(b).start()
 
+    for g in range(eager, groups):
+        over_peers(lambda k: send(g, k, 0, mine).start())
     taps = jnp.broadcast_to(kernel_row[...], (MB, pulses))
     base[...] = pltpu.roll(taps, 0, 1, stride=1, stride_axis=0).astype(BF16)
     for b in range(batches):
@@ -187,6 +189,7 @@
 
     parts = wide // CHUNK
     early = (groups - 1) * wide
+    lead = min(2, batches)
 
     def column_in(j, slot):
         return pltpu.make_async_copy(
@@ -203,30 +206,23 @@
             column_out, edge_az.at[:, pl.ds(j * CHUNK, CHUNK)], column_sem
         )
 
-    def send_back(k, row, rows, column, columns, sent_sem, here_sem):
+    def send_back(k, b, column, columns):
         peer = lax.rem(me + k, total)
         return pltpu.make_async_remote_copy(
-            src_ref=mag.at[pl.ds(peer * mine + row, rows), pl.ds(column, columns)],
-            dst_ref=rows_in.at[pl.ds(row, rows), pl.ds(me * width + column, columns)],
-            send_sem=sent_sem,
-            recv_sem=here_sem,
+            src_ref=mag.at[pl.ds(peer * mine + b * ROWS, ROWS), pl.ds(column, columns)],
+            dst_ref=rows_in.at[pl.ds(b * ROWS, ROWS), pl.ds(me * width + column, columns)],
+            send_sem=back_send.at[b, k],
+            recv_sem=back_recv.at[b, k],
             device_id=coords(peer, naz),
             device_id_type=MESH,
-        )
-
-    def send_early(k, column, columns):
-        return send_back(k, 0, mine, column, columns, early_send.at[k], early_recv.at[k])
-
-    def send_late(k, b):
-        return send_back(
-            k, b * ROWS, ROWS, early, wide, late_send.at[b, k], late_recv.at[b, k]
         )
 
     for g in range(groups):
         over_peers(lambda k: send(g, k, 0, mine).wait_recv())
         column_in(g * parts, 0).start()
-        if g + eager < groups:
-            over_peers(lambda k: send(g + eager, k, 0, mine).start())
+        if early and g + 1 == groups:
+            for b in range(lead):
+                over_peers(lambda k: send_back(k, b, 0, early).start())
         for part in range(parts):
             j = g * parts + part
             slot = part % 2
@@ -239,11 +235,9 @@
             size_out(j).start()
             if part + 1 == parts:
                 size_out(j).wait()
-                if g + 1 < groups:
-                    over_peers(lambda k: send_early(k, g * wide, wide).start())
-                else:
-                    for b in range(min(2, batches)):
-                        over_peers(lambda k: send_late(k, b).start())
+                if g + 1 == groups:
+                    for b in range(lead):
+                        over_peers(lambda k: send_back(k, b, early, wide).start())
             if j > 0:
                 column_back(j - 1).wait()
 
@@ -262,8 +256,6 @@
     own_rows.start()
     own_rows.wait()
     column_back(groups * parts - 1).wait()
-    if early:
-        over_peers(lambda k: send_early(k, 0, early).wait_recv())
 
     def turn(re, im):
         return -weights[...] * im, weights[...] * re
@@ -277,9 +269,9 @@
         return pltpu.make_async_copy(rows_out, edge_rg.at[pl.ds(b * ROWS, ROWS), :], rows_sem)
 
     for b in range(batches):
-        over_peers(lambda k: send_late(k, b).wait_recv())
-        if b + 2 < batches:
-            over_peers(lambda k: send_late(k, b + 2).start())
+        over_peers(lambda k: send_back(k, b, 0, width).wait_recv())
+        if b + lead < batches:
+            over_peers(lambda k: send_back(k, b + lead, 0, width).start())
         rows_load(b).start()
         rows_load(b).wait()
 
@@ -317,10 +309,8 @@
 
     for g in range(groups):
         over_peers(lambda k: send(g, k, 0, mine).wait_send())
-    if early:
-        over_peers(lambda k: send_early(k, 0, early).wait_send())
     for b in range(batches):
-        over_peers(lambda k: send_late(k, b).wait_send())
+        over_peers(lambda k: send_back(k, b, 0, width).wait_send())
 
 
 def butterflies(values, sign):
@@ -496,7 +486,7 @@
                 pltpu.VMEM((ROWS, bins), F32),
                 dma((2,)), dma((batches,)), dma((groups, total)), dma((groups, total)),
                 dma((2,)), dma, dma, dma,
-                dma((total,)), dma((total,)), dma((batches, total)), dma((batches, total)),
+                dma((batches, total)), dma((batches, total)),
             ],
             compiler_params=pltpu.CompilerParams(
                 collective_id=0, has_side_effects=True, vmem_limit_bytes=VMEM_LIMIT

time: 685 us -> 645 us (0.942)
  Pallas kernels: 648 us -> 606 us
    pallas_call x1, Pallas kernels: 648 us -> 606 us  [on_device(): pl.pallas_call(functools.partial(image_kernel, total, naz, batches, width...]
where the time goes in v3:
time: 645 us; the launch traced here: 643 us
  Pallas kernels  606 us (94%)
  local copies, waits for them, and re-layouts  30.1 us (5%)
    pallas_call x1, Pallas kernels, on_device(): pl.pallas_call(functools.partial(image_kernel, total, naz, batches, width...  606 us
    unnamed x8, local copies, waits for them, and re-layouts  23.2 us

profile of v3, /device:TPU:0, one launch (start us, length us, event | category | flops | bytes accessed | tf_op | source)
XLA Modules:
  0.0 643.0 jit_solution(5942012058826615491)
XLA Ops:
  0.6 1.2 slice.14
  1.8 0.8 slice.13
  2.6 0.1 reverse
  2.7 0.8 slice_add_fusion
  3.4 2.6 multiply_reduce_fusion
  6.0 0.1 reverse.1
  6.1 0.1 slice_negate_fusion
  6.1 0.7 concatenate.6
  6.8 1.1 slice.15
  7.9 0.4 reverse.2
  8.2 0.1 slice.19
  8.4 1.7 fusion
  10.1 0.1 reshape.19
  10.2 0.8 copy.22
  11.1 1.9 fusion.2
  12.9 0.1 cos.10
  13.0 0.1 copy.20
  13.1 0.1 sin.10
  13.2 0.1 copy.21
  13.4 0.8 pad_maximum_fusion.phase
  14.2 606.2 %image.1 = (bf16[2,2048,2048]{2,1,0:T(8,128)(2,1)}, bf16[2048,2048]{1,0:T(8,128)(2,1)}, bf16[64,65536]{1,0:T(8,128)(2,1)}, f32[2048,2048]{1,0:T(8,128)}, f32[64,65536]{1,0:T(8,128)}) custom-call(bf16[2,64,65536]{2,1,0:T(8,128)(2,1)} %raw.1, f32[2,256,256]{2,1,0:T(8,128)} %pad_maximum_fusion.phase, bf16[512,512]{1,0:T(8,128)(2,1)} %constant.31.clone.fl.gr, ...), custom_call_target="tpu_custom_call" | custom-call | tf_op jit(solution)/shard_map/image/image/pallas_call | solution.py:466
  620.4 12.7 %copy.25 = f32[2048,2048]{1,0:T(8,128)} copy(f32[2048,2048]{1,0:T(8,128)} %get-tuple-element.10) | data formatting | bytes 33554432
  633.1 3.7 copy-done
  636.8 6.2 copy.26
  (1 shorter events, 0.0 us)
Async XLA Ops:
  620.4 16.4 %copy-start = (f32[64,65536]{1,0:T(8,128)S(1)}, f32[64,65536]{1,0:T(8,128)}, u32[]{:S(2)}) copy-start(f32[64,65536]{1,0:T(8,128)} %get-tuple-element.11) | copy-start | bytes 50331652
